TPU v7x, 256 devices: a whole 4x4x8 slice. The times are simulated.
256 devices in a mesh: dp: 4 (over y), ty: 4 (over z_hi, core), tx: 16 (over z_lo, x).
Axes of the slice: x: 4, y: 4, z: 8 (z_hi: 2, z_lo: 4; z = z_hi * 4 + z_lo), core: 2. Of those that a mesh axis runs over, the one named last changes fastest.
Arguments:
- features: bfloat16 [4, 256, 1024, 128], P('dp', 'ty', 'tx'), may hold values from -6 to 6
- filter_one: bfloat16 [3, 3, 128, 128], P(None, None, None, 'dp'), may hold values from -0.1875 to 0.1875
- filter_two: bfloat16 [3, 3, 128, 128], P(None, None, None, 'dp'), may hold values from -0.1875 to 0.1875
- speedup: float32 [4, 256, 1024], P('dp', 'ty', 'tx'), may hold values from 0.5 to 2
- land_mask: int32 [4, 256, 1024], P('dp', 'ty', 'tx'), may hold values 0 or 1
- offsets: int32 [4, 2], P('dp'), may hold values from 0 to 1023
- upstream: bfloat16 [4, 256, 1024, 128], P('dp', 'ty', 'tx'), may hold values from -6 to 6
Outputs:
- output: bfloat16 [4, 256, 1024, 128], P('dp', 'ty', 'tx')
- grad_input: bfloat16 [4, 256, 1024, 128], P('dp', 'ty', 'tx')
- grad_one: float32 [3, 3, 128, 128], P(None, None, None, 'dp')
- grad_two: float32 [3, 3, 128, 128], P(None, None, None, 'dp')
All inputs are finite; a program needn't handle non-finite values. No bound on the sum of `land_mask` on one device may be relied on, other than what follows from the above.
Results may differ from a plain program's by a relative error of at most 0.014.
Values may be sent and summed in bfloat16 or wider, within the bound.
A program may use at most 64 MiB of HBM per device.

v0:
```python
import functools
import math

import jax
import jax.numpy as jnp
from jax import lax
from jax.experimental import pallas as pl
from jax.experimental.pallas import tpu as pltpu
from jax.sharding import PartitionSpec as P

MESH = pl.DeviceIdType.MESH
F32 = jnp.float32
BF16 = jnp.bfloat16

C = 128
T = 64
W = 80
PAIRS = 33
K = 6 * C
TAPS = 9 * C

DIRS = [(-1, -1), (-1, 0), (-1, 1), (0, -1), (0, 1), (1, -1), (1, 0), (1, 1)]


def dot(a, b):
    return jnp.dot(a, b, preferred_element_type=F32)


def kernel(
    sizes, crop, scale,
    features, filter_one, filter_two, speedup, mask, offsets, upstream,
    out, grad_in, grads_t,
    raw, tails, colsend, colrecv, speed_v, mask_v, terrain, factor, filt_v, wt, big,
    x_in, x_up, x_hid, x_gp, up_t, gp_t, pre, gh, rs, gf, gb, p1_recv, pieces_f, pieces_b, p2_recv,
    z_slots, g_full, g_out, out_v,
    local_sem, halo_s, halo_r, terr_s, terr_r, w_s, w_r, p1_s, p1_r, p2_s, p2_r, p4_s, p4_r, p5_s, p5_r, out_sem,
):
    n_dp, n_ty, n_tx = sizes
    n_x = 4
    n_zl = n_tx // n_x
    n_z = (n_ty // 2) * n_zl
    dp, ty, tx = lax.axis_index("dp"), lax.axis_index("ty"), lax.axis_index("tx")
    core, x = lax.rem(ty, 2), lax.rem(tx, n_x)
    zl = tx // n_x
    z = (ty // 2) * n_zl + zl

    def inside(dy, dx):
        ok = None
        if dy:
            ok = (ty > 0) if dy < 0 else (ty < n_ty - 1)
        if dx:
            okx = (tx > 0) if dx < 0 else (tx < n_tx - 1)
            ok = okx if ok is None else jnp.logical_and(ok, okx)
        return ok

    plane = [
        (lax.rem(dp + k // n_x, n_dp), ty, zl * n_x + lax.rem(x + k % n_x, n_x))
        for k in range(1, n_dp * n_x)
    ]

    def z_peer(k):
        to = lax.rem(z + k, n_z)
        return (dp, (to // n_zl) * 2 + core, lax.rem(to, n_zl) * n_x + x)

    z_peers = [z_peer(k) for k in range(1, n_z)]

    def mate(k):
        return (dp, (ty // 2) * 2 + lax.rem(core + k // n_x, 2), zl * n_x + lax.rem(x + k % n_x, n_x))

    mates = [mate(k) for k in range(1, 2 * n_x)]
    partner = mate(n_x)
    dp_peers = [(lax.rem(dp + k, n_dp), ty, tx) for k in range(1, n_dp)]

    def load(src, dst, i):
        copy = pltpu.make_async_copy(src, dst, local_sem.at[i])
        copy.start()
        return copy

    loads = [
        load(filter_one, filt_v.at[0], 0),
        load(filter_two, filt_v.at[1], 1),
        load(features.at[0], raw.at[0, pl.ds(2, T), pl.ds(0, T), :], 2),
        load(upstream.at[0], raw.at[1, pl.ds(2, T), pl.ds(0, T), :], 3),
        load(speedup.at[0], speed_v, 4),
        load(mask.at[0], mask_v, 5),
    ]

    barrier = pltpu.get_barrier_semaphore()
    for peer in plane + z_peers + mates:
        pl.semaphore_signal(barrier, inc=1, device_id=peer, device_id_type=MESH)
    for dy, dx in DIRS:
        @pl.when(inside(dy, dx))
        def _(dy=dy, dx=dx):
            pl.semaphore_signal(barrier, inc=1, device_id=(dp, ty + dy, tx + dx), device_id_type=MESH)
    rows_by = (ty > 0).astype(jnp.int32) + (ty < n_ty - 1).astype(jnp.int32)
    cols_by = (tx > 0).astype(jnp.int32) + (tx < n_tx - 1).astype(jnp.int32)
    awaited = len(plane) + len(z_peers) + len(mates) + rows_by + cols_by + rows_by * cols_by

    own = pl.ds(pl.multiple_of(dp * (C // n_dp), C // n_dp), C // n_dp)
    for f in range(2):
        loads[f].wait()
        for k in range(9):
            wt[f, k, own, :] = filt_v[f, k // 3, k % 3].astype(F32).T.astype(BF16)

    pl.semaphore_wait(barrier, awaited)

    def w_copy(f, k):
        return pltpu.make_async_remote_copy(
            src_ref=wt.at[f, :, own, :], dst_ref=wt.at[f, :, own, :],
            send_sem=w_s.at[f, k], recv_sem=w_r.at[f, k], device_id=dp_peers[k], device_id_type=MESH,
        )

    def w_arrival(f, k):
        rows = C // n_dp
        src = lax.rem(dp - (k + 1) + n_dp, n_dp)
        theirs = pl.ds(pl.multiple_of(src * rows, rows), rows)
        return pltpu.make_async_remote_copy(
            src_ref=wt.at[f, :, theirs, :], dst_ref=wt.at[f, :, theirs, :],
            send_sem=w_s.at[f, k], recv_sem=w_r.at[f, k], device_id=dp_peers[k], device_id_type=MESH,
        )

    for k in range(n_dp - 1):
        w_copy(0, k).start()

    loads[4].wait()
    loads[5].wait()
    local = jnp.where(mask_v[...] == 1, speed_v[...], jnp.float32(1.0))
    terrain[0, pl.ds(8, T), :] = jnp.concatenate([local, jnp.ones((T, C - T), F32)], axis=1)

    def terr_copy(i):
        dy, dx = DIRS[i]
        slot = {0: 0, 1: 1, -1: 2}[dx]
        src = {0: pl.ds(8, T), -1: pl.ds(8, 8), 1: pl.ds(T, 8)}[dy]
        dst = {0: pl.ds(8, T), -1: pl.ds(8 + T, 8), 1: pl.ds(0, 8)}[dy]
        return pltpu.make_async_remote_copy(
            src_ref=terrain.at[0, src, :], dst_ref=terrain.at[slot, dst, :],
            send_sem=terr_s.at[i], recv_sem=terr_r.at[i], device_id=(dp, ty + dy, tx + dx), device_id_type=MESH,
        )

    for i, d in enumerate(DIRS):
        @pl.when(inside(*d))
        def _(i=i):
            terr_copy(i).start()

    for n in range(2):
        loads[2 + n].wait()
        colsend[0, n] = raw[n, pl.ds(2, T), pl.ds(0, 16), :][:, 0:2, :]
        colsend[1, n] = raw[n, pl.ds(2, T), pl.ds(T - 16, 16), :][:, 14:16, :]

    def halo_copy(i):
        dy, dx = DIRS[i]
        if dx == 0:
            src = raw.at[:, pl.ds(2 if dy < 0 else T, 2), pl.ds(0, T), :]
            dst = raw.at[:, pl.ds(T + 2 if dy < 0 else 0, 2), pl.ds(0, T), :]
        else:
            s = {0: pl.ds(0, T), -1: pl.ds(0, 2), 1: pl.ds(T - 2, 2)}[dy]
            t = {0: pl.ds(2, T), -1: pl.ds(T + 2, 2), 1: pl.ds(0, 2)}[dy]
            src = colsend.at[0 if dx < 0 else 1, :, s]
            dst = colrecv.at[1 if dx < 0 else 0, :, t]
        return pltpu.make_async_remote_copy(
            src_ref=src, dst_ref=dst,
            send_sem=halo_s.at[i], recv_sem=halo_r.at[i], device_id=(dp, ty + dy, tx + dx), device_id_type=MESH,
        )

    for i, d in enumerate(DIRS):
        @pl.when(inside(*d))
        def _(i=i):
            halo_copy(i).start()
    for k in range(n_dp - 1):
        w_copy(1, k).start()

    for dy, dx in DIRS:
        @pl.when(jnp.logical_not(inside(dy, dx)))
        def _(dy=dy, dx=dx):
            if dx == 0:
                at = T + 2 if dy > 0 else 0
                raw[:, at:at + 2, 0:T, :] = jnp.zeros((2, 2, T, C), BF16)
            else:
                first, size = {0: (2, T), 1: (T + 2, 2), -1: (0, 2)}[dy]
                colrecv[1 if dx > 0 else 0, :, first:first + size] = jnp.zeros((2, size, 2, C), BF16)
    tails[...] = jnp.zeros_like(tails)

    def transpose_up(m, carry):
        pairs = []
        for u in range(2):
            r = 2 + 4 * m + 2 * u
            pairs.append(jnp.concatenate([raw[1, r, 0:T, :], raw[1, r + 1, 0:T, :]], axis=1))
        block = jnp.concatenate(pairs, axis=0)
        up_t[:, pl.ds(pl.multiple_of(m * C, C), C)] = block.T
        return carry

    lax.fori_loop(0, T // 4, transpose_up, 0)

    for i, d in enumerate(DIRS):
        @pl.when(inside(-d[0], -d[1]))
        def _(i=i):
            terr_copy(i).wait_recv()
    turned = [terrain[s].T for s in range(3)]
    cells = jnp.concatenate([turned[0][0:T], turned[2][0:8], turned[1][T - 8:T]], axis=0)
    lane = lax.broadcasted_iota(jnp.int32, (W, W), 1) - 8
    spot = lax.broadcasted_iota(jnp.int32, (W, W), 0)
    col = jnp.where(spot > T + 8, spot - W, spot)
    row_at, col_at = ty * T + lane, tx * T + col
    live = (row_at >= 0) & (row_at < crop[0]) & (col_at >= 0) & (col_at < crop[1]) & (col <= T) & (col >= -1)
    row_pos = (offsets[0, 0] + row_at).astype(F32)
    col_pos = (offsets[0, 1] + col_at).astype(F32)
    live = live & (lane >= -1) & (lane <= T)
    safe = jnp.where(live, cells, jnp.float32(0.0))
    fac = safe / (1.0 + row_pos / 512.0) / (1.0 + col_pos / 1024.0)
    fac = jnp.where(live, fac, jnp.float32(0.0))
    fac = jnp.concatenate([fac, jnp.zeros((W, C - W), F32)], axis=1)

    def spread(q, rolled):
        for t in range(2):
            factor[q, :, t * C:(t + 1) * C] = jnp.broadcast_to(rolled[:, 7 + t:8 + t], (W, C))
        return pltpu.roll(rolled, C - 2, axis=1)

    lax.fori_loop(0, PAIRS, spread, fac)

    def matrices(i, f, flip):
        for e in range(3):
            big[i, 0, e * C:(e + 1) * C, C:2 * C] = jnp.zeros((C, C), BF16)
            big[i, 1, (3 + e) * C:(4 + e) * C, 0:C] = jnp.zeros((C, C), BF16)
        for a in range(3):
            for e in range(3):
                block = wt[f, 3 * (2 - a) + 2 - e] if flip else wt[f, 3 * a + e].T
                for s in range(2):
                    r = a + s
                    at = (r % 2) * 3 * C + e * C
                    big[i, r // 2, at:at + C, s * C:(s + 1) * C] = block

    for k in range(n_dp - 1):
        w_arrival(0, k).wait_recv()
    matrices(0, 0, False)
    matrices(3, 0, True)

    for i, d in enumerate(DIRS):
        @pl.when(inside(-d[0], -d[1]))
        def _(i=i):
            halo_copy(i).wait_recv()

    for n in range(2):
        tails[n, :, 0:2, :] = colrecv[1, n].astype(F32)
        tails[n, :, 14:16, :] = colrecv[0, n].astype(F32)

    def shifted(q, carry):
        for n, dest in ((0, x_in), (1, x_up)):
            for t in range(2):
                cells = jnp.concatenate([raw[n, 2 * q + t, 0:T, :].astype(F32), tails[n, 2 * q + t]], axis=0)
                for e in range(3):
                    moved = cells if e == 1 else pltpu.roll(cells, 1 if e == 0 else W - 1, axis=0)
                    at = (3 * t + e) * C
                    dest[q, :, at:at + C] = moved.astype(BF16)
        return carry

    lax.fori_loop(0, PAIRS + 1, shifted, 0)
    x_in[PAIRS + 1] = jnp.zeros((W, K), BF16)

    def pair_conv(source, i, first, count, width):
        upper = source[pl.ds(first, count)].reshape(count * width, K)
        lower = source[pl.ds(first + 1, count)].reshape(count * width, K)
        return dot(upper, big[i, 0]) + dot(lower, big[i, 1])

    def conv_one(b, carry):
        pre[pl.ds(11 * b, 11)] = pair_conv(x_in, 0, 11 * b, 11, W).reshape(11, W, 2 * C)
        return carry

    lax.fori_loop(0, 3, conv_one, 0)

    for k in range(n_dp - 1):
        w_arrival(1, k).wait_recv()
    matrices(1, 1, True)
    matrices(2, 1, False)

    def conv_two(b, carry):
        gh[pl.ds(11 * b, 11)] = pair_conv(x_up, 1, 11 * b, 11, W).reshape(11, W, 2 * C)
        return carry

    lax.fori_loop(0, 3, conv_two, 0)

    def pointwise(q, carry):
        for t in range(2):
            lanes = slice(t * C, (t + 1) * C)
            value, fac_q = pre[q, :, lanes], factor[q, :, lanes]
            s = jax.nn.sigmoid(value)
            hid = value * s * fac_q
            gp = gh[q, :, lanes] * fac_q * s * (1.0 + value * (1.0 - s))
            for cells, dest in ((hid, x_hid), (gp, x_gp)):
                for e in range(3):
                    moved = cells if e == 1 else pltpu.roll(cells, 1 if e == 0 else W - 1, axis=0)
                    at = (3 * t + e) * C
                    dest[q, :, at:at + C] = moved[0:T].astype(BF16)
        return carry

    lax.fori_loop(0, PAIRS, pointwise, 0)
    x_gp[PAIRS] = jnp.zeros((T, K), BF16)

    def combine(f):
        half = 3 * C
        parts = (
            rs[0, 0:C, 0:half] + rs[0, C:, half:],
            rs[0, 0:C, half:] + rs[1, C:, 0:half],
            rs[1, 0:C, 0:half] + rs[1, C:, half:],
        )
        for a in range(3):
            part = (parts[a] * scale).reshape(C // 8, 8, half)
            gf[f, :, :, a * half:(a + 1) * half] = part
            gb[f, :, :, a * half:(a + 1) * half] = part.astype(BF16)

    for i in range(2):
        rs[i] = dot(up_t[...], x_hid[i:i + T // 2].reshape(T // 2 * T, K))
    combine(1)

    def transpose_gp(m, carry):
        pairs = []
        for u in range(2):
            q = 2 * m + u
            a = x_gp[q, :, C:2 * C]
            b = x_gp[q, :, 4 * C:5 * C]
            a = jnp.where(q == 0, jnp.zeros_like(a), a)
            b = jnp.where(q == PAIRS - 1, jnp.zeros_like(b), b)
            pairs.append(jnp.concatenate([a, b], axis=1))
        gp_t[:, pl.ds(pl.multiple_of(m * C, C), C)] = jnp.concatenate(pairs, axis=0).T
        return carry

    lax.fori_loop(0, (PAIRS + 1) // 2, transpose_gp, 0)
    for i in range(2):
        cells = x_in[i:i + PAIRS + 1, 0:T, :].reshape((PAIRS + 1) * T, K)
        rs[i] = dot(gp_t[...], cells)
    combine(0)

    p1 = pltpu.make_async_remote_copy(
        src_ref=gb.at[1 - core], dst_ref=p1_recv, send_sem=p1_s, recv_sem=p1_r, device_id=partner, device_id_type=MESH,
    )
    p1.start()

    def rows_out(source, i, dest, slot):
        def block(b, carry):
            y = pair_conv(source, i, 8 * b, 8, T).astype(BF16)
            out_v[slot, pl.ds(8 * b, 8), 0] = y[:, 0:C].reshape(8, T, C)
            out_v[slot, pl.ds(8 * b, 8), 1] = y[:, C:].reshape(8, T, C)
            return carry

        lax.fori_loop(0, 4, block, 0)
        copy = pltpu.make_async_copy(out_v.at[slot], dest, out_sem.at[slot])
        copy.start()
        return copy

    writes = [rows_out(x_hid, 2, out, 0)]

    p1.wait_recv()
    pieces = gf[core] + p1_recv[...].astype(F32)
    pieces_f[...] = pieces
    pieces_b[...] = pieces.astype(BF16)

    def p2_copy(k):
        to_dp, _, to_tx = plane[k]
        return pltpu.make_async_remote_copy(
            src_ref=pieces_b.at[to_dp * n_x + lax.rem(to_tx, n_x)], dst_ref=p2_recv.at[k],
            send_sem=p2_s.at[k], recv_sem=p2_r.at[k], device_id=plane[k], device_id_type=MESH,
        )

    p2 = [p2_copy(k) for k in range(len(plane))]
    for copy in p2:
        copy.start()

    writes.append(rows_out(x_gp, 3, grad_in, 1))

    for copy in p2:
        copy.wait_recv()
    mine = pieces_f[dp * n_x + x]
    for k in range(len(plane)):
        mine = mine + p2_recv[k].astype(F32)

    z_slots[z] = mine.astype(BF16)

    def p4_copy(k, at):
        return pltpu.make_async_remote_copy(
            src_ref=z_slots.at[at], dst_ref=z_slots.at[at],
            send_sem=p4_s.at[k], recv_sem=p4_r.at[k], device_id=z_peers[k], device_id_type=MESH,
        )

    p4 = [p4_copy(k, z) for k in range(len(z_peers))]
    for copy in p4:
        copy.start()
    for k in range(len(z_peers)):
        p4_copy(k, lax.rem(z - (k + 1) + n_z, n_z)).wait_recv()
    total = z_slots[0].astype(F32)
    for k in range(1, n_z):
        total = total + z_slots[k].astype(F32)

    g_full[core, x] = total.astype(BF16)

    def p5_copy(k, at_core, at_x):
        return pltpu.make_async_remote_copy(
            src_ref=g_full.at[at_core, at_x], dst_ref=g_full.at[at_core, at_x],
            send_sem=p5_s.at[k], recv_sem=p5_r.at[k], device_id=mates[k], device_id_type=MESH,
        )

    p5 = [p5_copy(k, core, x) for k in range(len(mates))]
    for copy in p5:
        copy.start()
    for k in range(len(mates)):
        dc, dx = (k + 1) // n_x, (k + 1) % n_x
        p5_copy(k, lax.rem(core + dc, 2), lax.rem(x - dx + n_x, n_x)).wait_recv()
    g_out[...] = g_full[...].astype(F32)
    last = pltpu.make_async_copy(g_out, grads_t, out_sem.at[2])
    last.start()

    for copy in p2 + p4 + p5:
        copy.wait_send()
    p1.wait_send()
    for f in range(2):
        for k in range(n_dp - 1):
            w_copy(f, k).wait_send()
    for i, d in enumerate(DIRS):
        @pl.when(inside(*d))
        def _(i=i):
            terr_copy(i).wait_send()
            halo_copy(i).wait_send()
    for copy in writes:
        copy.wait()
    last.wait()


def on_device(sizes, features, filter_one, filter_two, speedup, land_mask, offsets, upstream):
    n_dp, n_ty, n_tx = sizes
    n_x = 4
    n_z = n_ty * n_tx // (2 * n_x)
    rows = C // (n_dp * n_x)
    crop = (n_ty * T, n_tx * T)
    scale = 1.0 / math.sqrt(n_dp * crop[0] * crop[1])
    anywhere = pl.BlockSpec(memory_space=pl.ANY)
    vmem = pltpu.VMEM
    dma = pltpu.SemaphoreType.DMA
    n_plane, n_mates = n_dp * n_x - 1, 2 * n_x - 1
    scratch = [
        vmem((2, T + 4, W, C), BF16),
        vmem((2, T + 4, 16, C), F32),
        vmem((2, 2, T, 2, C), BF16),
        vmem((2, 2, T + 4, 2, C), BF16),
        vmem((T, T), F32),
        vmem((T, T), jnp.int32),
        vmem((3, W, C), F32),
        vmem((PAIRS, W, 2 * C), F32),
        vmem((2, 3, 3, C, C // n_dp), BF16),
        vmem((2, 9, C, C), BF16),
        vmem((4, 2, K, 2 * C), BF16),
        vmem((PAIRS + 2, W, K), BF16),
        vmem((PAIRS + 1, W, K), BF16),
        vmem((PAIRS, T, K), BF16),
        vmem((PAIRS + 1, T, K), BF16),
        vmem((2 * C, T * T // 2), BF16),
        vmem((2 * C, (PAIRS + 1) * T), BF16),
        vmem((PAIRS, W, 2 * C), F32),
        vmem((PAIRS, W, 2 * C), F32),
        vmem((2, 2 * C, K), F32),
        vmem((2, C // rows, rows, TAPS), F32),
        vmem((2, C // rows, rows, TAPS), BF16),
        vmem((C // rows, rows, TAPS), BF16),
        vmem((C // rows, rows, TAPS), F32),
        vmem((C // rows, rows, TAPS), BF16),
        vmem((n_plane, rows, TAPS), BF16),
        vmem((n_z, rows, TAPS), BF16),
        vmem((2, n_x, rows, TAPS), BF16),
        vmem((2, n_x, rows, TAPS), F32),
        vmem((2, T // 2, 2, T, C), BF16),
        dma((6,)),
        dma((8,)), dma((8,)),
        dma((8,)), dma((8,)),
        dma((2, n_dp - 1)), dma((2, n_dp - 1)),
        dma, dma,
        dma((n_plane,)), dma((n_plane,)),
        dma((n_z - 1,)), dma((n_z - 1,)),
        dma((n_mates,)), dma((n_mates,)),
        dma((3,)),
    ]
    out, grad_in, grads_t = pl.pallas_call(
        functools.partial(kernel, sizes, crop, scale),
        out_shape=(
            jax.ShapeDtypeStruct((T // 2, 2, T, C), BF16),
            jax.ShapeDtypeStruct((T // 2, 2, T, C), BF16),
            jax.ShapeDtypeStruct((2, n_x, rows, TAPS), F32),
        ),
        in_specs=[anywhere] * 5 + [pl.BlockSpec(memory_space=pltpu.SMEM), anywhere],
        out_specs=(anywhere,) * 3,
        scratch_shapes=scratch,
        compiler_params=pltpu.CompilerParams(
            collective_id=0, has_side_effects=True, vmem_limit_bytes=60 * 1024 * 1024
        ),
    )(features, filter_one, filter_two, speedup, land_mask, offsets, upstream)
    grads = grads_t.reshape(2, C // n_dp, 9, C).transpose(0, 2, 3, 1).reshape(2, 3, 3, C, C // n_dp)
    return out.reshape(1, T, T, C), grad_in.reshape(1, T, T, C), grads[0], grads[1]


def solution(mesh):
    tile = P("dp", "ty", "tx", None)
    filters = P(None, None, None, "dp")
    plane = P("dp", "ty", "tx")
    sizes = (mesh.shape["dp"], mesh.shape["ty"], mesh.shape["tx"])
    return jax.shard_map(
        functools.partial(on_device, sizes),
        mesh=mesh,
        in_specs=(tile, filters, filters, plane, plane, P("dp", None), tile),
        out_specs=(tile, tile, filters, filters),
        check_vma=False,
    )
```

profile of v0, /device:TPU:1, one launch (start us, length us, event | category | flops | bytes accessed | tf_op | source)
XLA Modules:
  0.0 63.9 jit_solution(1766007585594617254)
XLA Ops:
  0.6 0.0 copy-start.2
  0.6 1.8 %copy.19.filter_one = bf16[3,3,128,32]{3,2,1,0:T(8,128)(2,1)} copy(bf16[3,3,128,32]{2,3,1,0:T(8,128)(2,1)} %param.8) | data formatting | bytes 147456 | tf_op args[1]
  2.4 0.0 copy-done.2
  2.4 0.9 %copy.20.filter_two = bf16[3,3,128,32]{3,2,1,0:T(8,128)(2,1)} copy(bf16[3,3,128,32]{2,3,1,0:T(8,128)(2,1)S(1)} %copy-done.2) | data formatting | bytes 147456 | tf_op args[2]
  3.3 55.5 %shard_map.102 = (bf16[32,2,64,128]{3,2,1,0:T(8,128)(2,1)}, bf16[32,2,64,128]{3,2,1,0:T(8,128)(2,1)}, f32[2,4,8,1152]{3,2,1,0:T(8,128)}) custom-call(bf16[1,64,64,128]{3,2,1,0:T(8,128)(2,1)} %features.1, bf16[3,3,128,32]{3,2,1,0:T(8,128)(2,1)} %copy.19.filter_one, bf16[3,3,128,32]{3,2,1,0:T(8,128)(2,1)} %copy.20.filter_two, f32[1,64,64]{2,1,0:T(8,128)} %speedup.1, ...), custom_call_target="tpu_custom_call" | custom-call | tf_op jit(solution)/shard_map/pallas_call | solution.py:478
  58.9 1.0 %reshape.24 = f32[2,32,9,128]{3,2,1,0:T(8,128)S(1)} reshape(f32[2,4,8,1152]{3,2,1,0:T(8,128)} %get-tuple-element.9) | data formatting | bytes 589824 | tf_op jit(solution)/shard_map/reshape | solution.py:492
  59.9 0.0 copy-start.1
  59.9 0.7 %copy.22 = f32[1,9,128,32]{2,3,1,0:T(8,128)} copy(f32[1,9,128,32]{2,1,3,0:T(8,128)S(1)} %get-tuple-element.14) | data formatting | bytes 294912 | tf_op jit(solution)/shard_map/slice | solution.py:493
  60.6 0.7 %copy.21 = f32[1,9,128,32]{2,3,1,0:T(8,128)} copy(f32[1,9,128,32]{2,1,3,0:T(8,128)S(1)} %get-tuple-element.15) | data formatting | bytes 294912 | tf_op jit(solution)/shard_map/slice | solution.py:493
  61.3 0.0 copy-done.1
  61.3 0.0 copy-start
  61.3 1.0 %copy.25 = bf16[1,64,64,128]{3,2,1,0:T(8,128)(2,1)} copy(bf16[1,64,64,128]{3,2,1,0:T(8,128)(2,1)S(1)} %bitcast.9) | data formatting | bytes 2097152
  62.3 0.6 copy-done
  62.9 1.0 %copy.26 = bf16[1,64,64,128]{3,2,1,0:T(8,128)(2,1)} copy(bf16[1,64,64,128]{3,2,1,0:T(8,128)(2,1)S(1)} %bitcast.8) | data formatting | bytes 2097152
  (1 shorter events, 0.0 us)
Async XLA Ops:
  0.6 1.8 %copy-start.2 = (bf16[3,3,128,32]{2,3,1,0:T(8,128)(2,1)S(1)}, bf16[3,3,128,32]{2,3,1,0:T(8,128)(2,1)}, u32[]{:S(2)}) copy-start(bf16[3,3,128,32]{2,3,1,0:T(8,128)(2,1)} %param.9) | copy-start | bytes 221188
  59.9 1.5 %copy-start.1 = (bf16[32,2,64,128]{3,2,1,0:T(8,128)(2,1)S(1)}, bf16[32,2,64,128]{3,2,1,0:T(8,128)(2,1)}, u32[]{:S(2)}) copy-start(bf16[32,2,64,128]{3,2,1,0:T(8,128)(2,1)} %get-tuple-element.7) | copy-start | bytes 3145732
  61.3 1.6 %copy-start = (bf16[32,2,64,128]{3,2,1,0:T(8,128)(2,1)S(1)}, bf16[32,2,64,128]{3,2,1,0:T(8,128)(2,1)}, u32[]{:S(2)}) copy-start(bf16[32,2,64,128]{3,2,1,0:T(8,128)(2,1)} %get-tuple-element.8) | copy-start | bytes 3145732
where the time goes:
time: 64.2 us; the launch traced here: 63.9 us
  Pallas kernels  55.5 us (86%)
  local copies, waits for them, and re-layouts  7.74 us (12%)
  between operations  0.68 us (1%)
    pallas_call x1, Pallas kernels, on_device(): pl.pallas_call(functools.partial(kernel, sizes, crop, scale), out_shape=(...  55.5 us
    unnamed x10, local copies, waits for them, and re-layouts  5.28 us

commit v1 on v0

v1 whole, which is shorter than its diff:
```python
import functools
import math

import jax
import jax.numpy as jnp
from jax import lax
from jax.experimental import pallas as pl
from jax.experimental.pallas import tpu as pltpu
from jax.sharding import PartitionSpec as P

MESH = pl.DeviceIdType.MESH
F32 = jnp.float32
BF16 = jnp.bfloat16

C = 128
T = 64
W = 80
PAIRS = 33
K = 6 * C
TAPS = 9 * C

DIRS = [(-1, -1), (-1, 0), (-1, 1), (0, -1), (0, 1), (1, -1), (1, 0), (1, 1)]


def dot(a, b):
    return jnp.dot(a, b, preferred_element_type=F32)


def kernel(
    sizes, crop, scale,
    features, filter_one, filter_two, speedup, mask, offsets, upstream,
    out, grad_in, grad_one, grad_two,
    raw, tails, colsend, colrecv, speed_v, mask_v, off_v, terrain, factor, wt, big,
    x_in, x_up, x_hid, x_gp, up_t, gp_t, pre, gh, rs, gf, gb, p1_recv, pieces_f, pieces_b, p2_recv,
    z_slots, g_full, g_out, out_v,
    local_sem, rows_s, rows_r, halo_s, halo_r, terr_s, terr_r, w_s, w_r, p1_s, p1_r, p2_s, p2_r, p4_s, p4_r, p5_s, p5_r, out_sem,
):
    n_dp, n_ty, n_tx = sizes
    n_x = 4
    n_zl = n_tx // n_x
    n_z = (n_ty // 2) * n_zl
    dp, ty, tx = lax.axis_index("dp"), lax.axis_index("ty"), lax.axis_index("tx")
    core, x = lax.rem(ty, 2), lax.rem(tx, n_x)
    zl = tx // n_x
    z = (ty // 2) * n_zl + zl

    def inside(dy, dx):
        ok = None
        if dy:
            ok = (ty > 0) if dy < 0 else (ty < n_ty - 1)
        if dx:
            okx = (tx > 0) if dx < 0 else (tx < n_tx - 1)
            ok = okx if ok is None else jnp.logical_and(ok, okx)
        return ok

    plane = [
        (lax.rem(dp + k // n_x, n_dp), ty, zl * n_x + lax.rem(x + k % n_x, n_x))
        for k in range(1, n_dp * n_x)
    ]

    def z_peer(k):
        to = lax.rem(z + k, n_z)
        return (dp, (to // n_zl) * 2 + core, lax.rem(to, n_zl) * n_x + x)

    z_peers = [z_peer(k) for k in range(1, n_z)]

    def mate(k):
        return (dp, (ty // 2) * 2 + lax.rem(core + k // n_x, 2), zl * n_x + lax.rem(x + k % n_x, n_x))

    mates = [mate(k) for k in range(1, 2 * n_x)]
    partner = mate(n_x)
    dp_peers = [(lax.rem(dp + k, n_dp), ty, tx) for k in range(1, n_dp)]

    def load(src, dst, i):
        copy = pltpu.make_async_copy(src, dst, local_sem.at[i])
        copy.start()
        return copy

    rows = C // n_dp
    own = pl.ds(pl.multiple_of(dp * rows, rows), rows)
    filters = (filter_one, filter_two)
    loads = [
        load(features.at[0], raw.at[0, pl.ds(2, T), pl.ds(0, T), :], 0),
        load(upstream.at[0], raw.at[1, pl.ds(2, T), pl.ds(0, T), :], 1),
        load(speedup.at[0], speed_v, 2),
        load(mask.at[0], mask_v, 3),
        load(filter_one, wt.at[0, :, own, :], 4),
        load(filter_two, wt.at[1, :, own, :], 5),
        load(offsets, off_v, 6),
    ]

    barrier = pltpu.get_barrier_semaphore()
    for peer in plane + z_peers + mates:
        pl.semaphore_signal(barrier, inc=1, device_id=peer, device_id_type=MESH)
    for dy, dx in DIRS:
        @pl.when(inside(dy, dx))
        def _(dy=dy, dx=dx):
            pl.semaphore_signal(barrier, inc=1, device_id=(dp, ty + dy, tx + dx), device_id_type=MESH)
    rows_by = (ty > 0).astype(jnp.int32) + (ty < n_ty - 1).astype(jnp.int32)
    cols_by = (tx > 0).astype(jnp.int32) + (tx < n_tx - 1).astype(jnp.int32)
    awaited = len(plane) + len(z_peers) + len(mates) + rows_by + cols_by + rows_by * cols_by

    loads[2].wait()
    loads[3].wait()
    local = jnp.where(mask_v[...] == 1, speed_v[...], jnp.float32(1.0))
    terrain[0, pl.ds(8, T), :] = jnp.concatenate([local, jnp.ones((T, C - T), F32)], axis=1)
    for n in range(2):
        loads[n].wait()
        colsend[0, n] = raw[n, pl.ds(2, T), pl.ds(0, 16), :][:, 0:2, :]
        colsend[1, n] = raw[n, pl.ds(2, T), pl.ds(T - 16, 16), :][:, 14:16, :]

    pl.semaphore_wait(barrier, awaited)

    def w_copy(f, k):
        return pltpu.make_async_remote_copy(
            src_ref=filters[f], dst_ref=wt.at[f, :, own, :],
            send_sem=w_s.at[f, k], recv_sem=w_r.at[f, k], device_id=dp_peers[k], device_id_type=MESH,
        )

    def w_arrival(f, k):
        src = lax.rem(dp - (k + 1) + n_dp, n_dp)
        theirs = pl.ds(pl.multiple_of(src * rows, rows), rows)
        return pltpu.make_async_remote_copy(
            src_ref=filters[f], dst_ref=wt.at[f, :, theirs, :],
            send_sem=w_s.at[f, k], recv_sem=w_r.at[f, k], device_id=dp_peers[k], device_id_type=MESH,
        )

    def rows_copy(i, n):
        dy = DIRS[i][0]
        return pltpu.make_async_remote_copy(
            src_ref=(features, upstream)[n].at[0, pl.ds(0 if dy < 0 else T - 2, 2)],
            dst_ref=raw.at[n, pl.ds(T + 2 if dy < 0 else 0, 2), pl.ds(0, T), :],
            send_sem=rows_s.at[i // 4, n], recv_sem=rows_r.at[i // 4, n],
            device_id=(dp, ty + dy, tx), device_id_type=MESH,
        )

    def halo_copy(i):
        dy, dx = DIRS[i]
        s = {0: pl.ds(0, T), -1: pl.ds(0, 2), 1: pl.ds(T - 2, 2)}[dy]
        t = {0: pl.ds(2, T), -1: pl.ds(T + 2, 2), 1: pl.ds(0, 2)}[dy]
        return pltpu.make_async_remote_copy(
            src_ref=colsend.at[0 if dx < 0 else 1, :, s], dst_ref=colrecv.at[1 if dx < 0 else 0, :, t],
            send_sem=halo_s.at[i], recv_sem=halo_r.at[i], device_id=(dp, ty + dy, tx + dx), device_id_type=MESH,
        )

    def rim_copies(i):
        return [rows_copy(i, n) for n in range(2)] if DIRS[i][1] == 0 else [halo_copy(i)]

    def terr_copy(i):
        dy, dx = DIRS[i]
        slot = {0: 0, 1: 1, -1: 2}[dx]
        src = {0: pl.ds(8, T), -1: pl.ds(8, 8), 1: pl.ds(T, 8)}[dy]
        dst = {0: pl.ds(8, T), -1: pl.ds(8 + T, 8), 1: pl.ds(0, 8)}[dy]
        return pltpu.make_async_remote_copy(
            src_ref=terrain.at[0, src, :], dst_ref=terrain.at[slot, dst, :],
            send_sem=terr_s.at[i], recv_sem=terr_r.at[i], device_id=(dp, ty + dy, tx + dx), device_id_type=MESH,
        )

    beside, above = (3, 4), (0, 1, 2, 5, 6, 7)
    for i in (1, 6) + beside:
        @pl.when(inside(*DIRS[i]))
        def _(i=i):
            for copy in rim_copies(i):
                copy.start()
    for i, d in enumerate(DIRS):
        @pl.when(inside(*d))
        def _(i=i):
            terr_copy(i).start()
    for k in range(n_dp - 1):
        w_copy(0, k).start()
    for i in (0, 2, 5, 7):
        @pl.when(inside(*DIRS[i]))
        def _(i=i):
            halo_copy(i).start()

    for k in range(n_dp - 1):
        w_copy(1, k).start()

    for dy, dx in DIRS:
        @pl.when(jnp.logical_not(inside(dy, dx)))
        def _(dy=dy, dx=dx):
            if dx == 0:
                at = T + 2 if dy > 0 else 0
                raw[:, at:at + 2, 0:T, :] = jnp.zeros((2, 2, T, C), BF16)
            else:
                first, size = {0: (2, T), 1: (T + 2, 2), -1: (0, 2)}[dy]
                colrecv[1 if dx > 0 else 0, :, first:first + size] = jnp.zeros((2, size, 2, C), BF16)
    tails[...] = jnp.zeros_like(tails)

    def transpose_up(m, carry):
        pairs = []
        for u in range(2):
            r = 2 + 4 * m + 2 * u
            pairs.append(jnp.concatenate([raw[1, r, 0:T, :], raw[1, r + 1, 0:T, :]], axis=1))
        block = jnp.concatenate(pairs, axis=0)
        up_t[:, pl.ds(pl.multiple_of(m * C, C), C)] = block.T
        return carry

    lax.fori_loop(0, T // 4, transpose_up, 0)

    def matrices(i, f, flip):
        for e in range(3):
            big[i, 0, e * C:(e + 1) * C, C:2 * C] = jnp.zeros((C, C), BF16)
            big[i, 1, (3 + e) * C:(4 + e) * C, 0:C] = jnp.zeros((C, C), BF16)
        for a in range(3):
            for e in range(3):
                block = wt[f, 3 * (2 - a) + 2 - e] if flip else wt[f, 3 * a + e].T
                for s in range(2):
                    r = a + s
                    at = (r % 2) * 3 * C + e * C
                    big[i, r // 2, at:at + C, s * C:(s + 1) * C] = block

    def await_rim(which):
        for i in which:
            @pl.when(inside(-DIRS[i][0], -DIRS[i][1]))
            def _(i=i):
                for copy in rim_copies(i):
                    copy.wait_recv()

    def shifted(q, carry):
        for n, dest in ((0, x_in), (1, x_up)):
            for t in range(2):
                cells = jnp.concatenate([raw[n, 2 * q + t, 0:T, :].astype(F32), tails[n, 2 * q + t]], axis=0)
                for e in range(3):
                    moved = cells if e == 1 else pltpu.roll(cells, 1 if e == 0 else W - 1, axis=0)
                    at = (3 * t + e) * C
                    dest[q, :, at:at + C] = moved.astype(BF16)
        return carry

    def fill_tails(first, size):
        for n in range(2):
            tails[n, first:first + size, 0:2, :] = colrecv[1, n, first:first + size].astype(F32)
            tails[n, first:first + size, 14:16, :] = colrecv[0, n, first:first + size].astype(F32)

    await_rim(beside)
    fill_tails(2, T)
    lax.fori_loop(1, PAIRS, shifted, 0)
    for i, d in enumerate(DIRS):
        @pl.when(inside(-d[0], -d[1]))
        def _(i=i):
            terr_copy(i).wait_recv()
    turned = [terrain[s].T for s in range(3)]
    cells = jnp.concatenate([turned[0][0:T], turned[2][0:8], turned[1][T - 8:T]], axis=0)
    lane = lax.broadcasted_iota(jnp.int32, (W, W), 1) - 8
    spot = lax.broadcasted_iota(jnp.int32, (W, W), 0)
    col = jnp.where(spot > T + 8, spot - W, spot)
    row_at, col_at = ty * T + lane, tx * T + col
    live = (row_at >= 0) & (row_at < crop[0]) & (col_at >= 0) & (col_at < crop[1]) & (col <= T) & (col >= -1)
    loads[6].wait()
    row_pos = (off_v[0, 0] + row_at).astype(F32)
    col_pos = (off_v[0, 1] + col_at).astype(F32)
    live = live & (lane >= -1) & (lane <= T)
    safe = jnp.where(live, cells, jnp.float32(0.0))
    fac = safe / (1.0 + row_pos / 512.0) / (1.0 + col_pos / 1024.0)
    fac = jnp.where(live, fac, jnp.float32(0.0))
    fac = jnp.concatenate([fac, jnp.zeros((W, C - W), F32)], axis=1)

    for q in range(PAIRS):
        for t in range(2):
            at = 2 * q + 7 + t
            factor[q, :, t * C:(t + 1) * C] = jnp.broadcast_to(fac[:, at:at + 1], (W, C))

    loads[4].wait()
    loads[5].wait()
    for k in range(n_dp - 1):
        w_arrival(0, k).wait_recv()
    matrices(0, 0, False)

    def pair_conv(source, i, first, count, width):
        upper = source[pl.ds(first, count)].reshape(count * width, K)
        lower = source[pl.ds(first + 1, count)].reshape(count * width, K)
        return dot(upper, big[i, 0]) + dot(lower, big[i, 1])

    def main_conv(source, i, dest):
        def block(b, carry):
            first = 10 * b + 1
            dest[pl.ds(first, 10)] = pair_conv(source, i, first, 10, W).reshape(10, W, 2 * C)
            return carry

        lax.fori_loop(0, 3, block, 0)

    ends = (0, PAIRS - 2, PAIRS - 1)

    def end_conv(source, i, dest):
        upper = jnp.concatenate([source[q] for q in ends], axis=0)
        lower = jnp.concatenate([source[q + 1] for q in ends], axis=0)
        both = dot(upper, big[i, 0]) + dot(lower, big[i, 1])
        for k, q in enumerate(ends):
            dest[q] = both[k * W:(k + 1) * W]

    main_conv(x_in, 0, pre)
    for k in range(n_dp - 1):
        w_arrival(1, k).wait_recv()
    matrices(1, 1, True)
    main_conv(x_up, 1, gh)

    await_rim(above)
    fill_tails(0, 2)
    fill_tails(T + 2, 2)
    shifted(0, 0)
    shifted(PAIRS, 0)
    x_in[PAIRS + 1] = jnp.zeros((W, K), BF16)
    end_conv(x_in, 0, pre)
    end_conv(x_up, 1, gh)

    def pointwise(q, carry):
        for t in range(2):
            lanes = slice(t * C, (t + 1) * C)
            value, fac_q = pre[q, :, lanes], factor[q, :, lanes]
            s = jax.nn.sigmoid(value)
            hid = value * s * fac_q
            gp = gh[q, :, lanes] * fac_q * s * (1.0 + value * (1.0 - s))
            for cells, dest in ((hid, x_hid), (gp, x_gp)):
                for e in range(3):
                    moved = cells if e == 1 else pltpu.roll(cells, 1 if e == 0 else W - 1, axis=0)
                    at = (3 * t + e) * C
                    dest[q, :, at:at + C] = moved[0:T].astype(BF16)
        return carry

    lax.fori_loop(0, PAIRS, pointwise, 0)
    x_gp[PAIRS] = jnp.zeros((T, K), BF16)

    def combine(f):
        half = 3 * C
        parts = (
            rs[0, 0:C, 0:half] + rs[0, C:, half:],
            rs[0, 0:C, half:] + rs[1, C:, 0:half],
            rs[1, 0:C, 0:half] + rs[1, C:, half:],
        )
        for a in range(3):
            part = (parts[a] * scale).reshape(C // 8, 8, half)
            gf[f, :, :, a * half:(a + 1) * half] = part
            gb[f, :, :, a * half:(a + 1) * half] = part.astype(BF16)

    p1 = pltpu.make_async_remote_copy(
        src_ref=gb.at[1 - core], dst_ref=p1_recv, send_sem=p1_s, recv_sem=p1_r, device_id=partner, device_id_type=MESH,
    )

    def p2_copy(k):
        to_dp, _, to_tx = plane[k]
        return pltpu.make_async_remote_copy(
            src_ref=pieces_b.at[to_dp * n_x + lax.rem(to_tx, n_x)], dst_ref=p2_recv.at[k],
            send_sem=p2_s.at[k], recv_sem=p2_r.at[k], device_id=plane[k], device_id_type=MESH,
        )

    def p4_copy(k, at):
        return pltpu.make_async_remote_copy(
            src_ref=z_slots.at[at], dst_ref=z_slots.at[at],
            send_sem=p4_s.at[k], recv_sem=p4_r.at[k], device_id=z_peers[k], device_id_type=MESH,
        )

    def p5_copy(k, at_core, at_x):
        return pltpu.make_async_remote_copy(
            src_ref=g_full.at[at_core, at_x], dst_ref=g_full.at[at_core, at_x],
            send_sem=p5_s.at[k], recv_sem=p5_r.at[k], device_id=mates[k], device_id_type=MESH,
        )

    def p2_start():
        p1.wait_recv()
        pieces = gf[core] + p1_recv[...].astype(F32)
        pieces_f[...] = pieces
        pieces_b[...] = pieces.astype(BF16)
        for k in range(len(plane)):
            p2_copy(k).start()

    def p4_start():
        for k in range(len(plane)):
            p2_copy(k).wait_recv()
        mine = pieces_f[dp * n_x + x]
        for k in range(len(plane)):
            mine = mine + p2_recv[k].astype(F32)
        z_slots[z] = mine.astype(BF16)
        for k in range(len(z_peers)):
            p4_copy(k, z).start()

    def p5_start():
        for k in range(len(z_peers)):
            p4_copy(k, lax.rem(z - (k + 1) + n_z, n_z)).wait_recv()
        total = z_slots[0].astype(F32)
        for k in range(1, n_z):
            total = total + z_slots[k].astype(F32)
        g_full[core, x] = total.astype(BF16)
        for k in range(len(mates)):
            p5_copy(k, core, x).start()

    def on_core(which, step):
        @pl.when(core == which)
        def _():
            step()

    for m in range((PAIRS + 1) // 2):
        pairs = []
        for q in (2 * m, 2 * m + 1):
            a, b = x_gp[q, :, C:2 * C], x_gp[q, :, 4 * C:5 * C]
            a = jnp.zeros_like(a) if q == 0 else a
            b = jnp.zeros_like(b) if q == PAIRS - 1 else b
            pairs.append(jnp.concatenate([a, b], axis=1))
        gp_t[:, m * C:(m + 1) * C] = jnp.concatenate(pairs, axis=0).T

    for i in range(2):
        rs[i] = dot(up_t[...], x_hid[i:i + T // 2].reshape(T // 2 * T, K))
    combine(1)
    on_core(0, p1.start)

    for i in range(2):
        if i == 1:
            on_core(1, p2_start)
        cells = x_in[i:i + PAIRS + 1, 0:T, :].reshape((PAIRS + 1) * T, K)
        rs[i] = dot(gp_t[...], cells)
    combine(0)
    on_core(1, p1.start)

    matrices(2, 1, False)
    matrices(3, 0, True)

    def rows_out(source, i, slot, first):
        def block(b, carry):
            y = pair_conv(source, i, 8 * b, 8, T).astype(BF16)
            out_v[slot, pl.ds(8 * b, 8), 0] = y[:, 0:C].reshape(8, T, C)
            out_v[slot, pl.ds(8 * b, 8), 1] = y[:, C:].reshape(8, T, C)
            return carry

        lax.fori_loop(first, first + 2, block, 0)

    on_core(0, p2_start)
    on_core(1, p4_start)
    rows_out(x_hid, 2, 0, 0)
    rows_out(x_hid, 2, 0, 2)
    writes = [pltpu.make_async_copy(out_v.at[0], out, out_sem.at[0])]
    writes[0].start()
    on_core(1, p5_start)
    rows_out(x_gp, 3, 1, 0)
    on_core(0, p4_start)
    rows_out(x_gp, 3, 1, 2)
    writes.append(pltpu.make_async_copy(out_v.at[1], grad_in, out_sem.at[1]))
    writes[1].start()
    on_core(0, p5_start)

    for k in range(len(mates)):
        dc, dx = (k + 1) // n_x, (k + 1) % n_x
        p5_copy(k, lax.rem(core + dc, 2), lax.rem(x - dx + n_x, n_x)).wait_recv()
    piece = C // (n_dp * n_x)
    for f, dest in enumerate((grad_one, grad_two)):
        for part in range(n_x):
            for k in range(9):
                g_out[f, k, part * piece:(part + 1) * piece, :] = g_full[f, part, :, k * C:(k + 1) * C].astype(F32)
        writes.append(pltpu.make_async_copy(g_out.at[f], dest, out_sem.at[2 + f]))
        writes[-1].start()

    for k in range(len(plane)):
        p2_copy(k).wait_send()
    for k in range(len(z_peers)):
        p4_copy(k, z).wait_send()
    for k in range(len(mates)):
        p5_copy(k, core, x).wait_send()
    p1.wait_send()
    for f in range(2):
        for k in range(n_dp - 1):
            w_copy(f, k).wait_send()
    for i, d in enumerate(DIRS):
        @pl.when(inside(*d))
        def _(i=i):
            terr_copy(i).wait_send()
            for copy in rim_copies(i):
                copy.wait_send()
    for copy in writes:
        copy.wait()


def by_output(filters):
    return filters.transpose(0, 1, 3, 2).reshape(9, filters.shape[3], C)


def by_input(grads):
    return grads.reshape(3, 3, grads.shape[1], C).transpose(0, 1, 3, 2)


def placed(*refs):
    sources, dests, held, (in_sem, out_sem) = refs[0:4], refs[4:8], refs[8:12], refs[12:14]
    parts = []
    for source, dest, mid in zip(sources, dests, held):
        count = 4 if source.shape[0] % 4 == 0 else 1
        step = source.shape[0] // count
        parts += [(source, dest, mid, pl.ds(p * step, step)) for p in range(count)]
    reads = [
        pltpu.make_async_copy(source.at[at], mid.at[at], in_sem.at[i]) for i, (source, dest, mid, at) in enumerate(parts)
    ]
    writes = [
        pltpu.make_async_copy(mid.at[at], dest.at[at], out_sem.at[i]) for i, (source, dest, mid, at) in enumerate(parts)
    ]
    for copy in reads:
        copy.start()
    for read, write in zip(reads, writes):
        read.wait()
        write.start()
    for copy in writes:
        copy.wait()


def on_device(sizes, features, filter_one, filter_two, speedup, land_mask, offsets, upstream):
    n_dp, n_ty, n_tx = sizes
    n_x = 4
    n_z = n_ty * n_tx // (2 * n_x)
    rows = C // (n_dp * n_x)
    crop = (n_ty * T, n_tx * T)
    scale = 1.0 / math.sqrt(n_dp * crop[0] * crop[1])
    anywhere = pl.BlockSpec(memory_space=pl.ANY)
    vmem = pltpu.VMEM
    dma = pltpu.SemaphoreType.DMA
    n_plane, n_mates = n_dp * n_x - 1, 2 * n_x - 1
    scratch = [
        vmem((2, T + 4, W, C), BF16),
        vmem((2, T + 4, 16, C), F32),
        vmem((2, 2, T, 2, C), BF16),
        vmem((2, 2, T + 4, 2, C), BF16),
        vmem((T, T), F32),
        vmem((T, T), jnp.int32),
        pltpu.SMEM((1, 2), jnp.int32),
        vmem((3, W, C), F32),
        vmem((PAIRS, W, 2 * C), F32),
        vmem((2, 9, C, C), BF16),
        vmem((4, 2, K, 2 * C), BF16),
        vmem((PAIRS + 2, W, K), BF16),
        vmem((PAIRS + 1, W, K), BF16),
        vmem((PAIRS, T, K), BF16),
        vmem((PAIRS + 1, T, K), BF16),
        vmem((2 * C, T * T // 2), BF16),
        vmem((2 * C, (PAIRS + 1) * T), BF16),
        vmem((PAIRS, W, 2 * C), F32),
        vmem((PAIRS, W, 2 * C), F32),
        vmem((2, 2 * C, K), F32),
        vmem((2, C // rows, rows, TAPS), F32),
        vmem((2, C // rows, rows, TAPS), BF16),
        vmem((C // rows, rows, TAPS), BF16),
        vmem((C // rows, rows, TAPS), F32),
        vmem((C // rows, rows, TAPS), BF16),
        vmem((n_plane, rows, TAPS), BF16),
        vmem((n_z, rows, TAPS), BF16),
        vmem((2, n_x, rows, TAPS), BF16),
        vmem((2, 9, C // n_dp, C), F32),
        vmem((2, T // 2, 2, T, C), BF16),
        dma((7,)),
        dma((2, 2)), dma((2, 2)),
        dma((8,)), dma((8,)),
        dma((8,)), dma((8,)),
        dma((2, n_dp - 1)), dma((2, n_dp - 1)),
        dma, dma,
        dma((n_plane,)), dma((n_plane,)),
        dma((n_z - 1,)), dma((n_z - 1,)),
        dma((n_mates,)), dma((n_mates,)),
        dma((4,)),
    ]
    out, grad_in, grad_one, grad_two = pl.pallas_call(
        functools.partial(kernel, sizes, crop, scale),
        out_shape=(
            jax.ShapeDtypeStruct((T // 2, 2, T, C), BF16),
            jax.ShapeDtypeStruct((T // 2, 2, T, C), BF16),
            jax.ShapeDtypeStruct((9, C // n_dp, C), F32),
            jax.ShapeDtypeStruct((9, C // n_dp, C), F32),
        ),
        in_specs=[anywhere] * 7,
        out_specs=(anywhere,) * 4,
        scratch_shapes=scratch,
        compiler_params=pltpu.CompilerParams(
            collective_id=0, has_side_effects=True, vmem_limit_bytes=60 * 1024 * 1024
        ),
    )(features, by_output(filter_one), by_output(filter_two), speedup, land_mask, offsets, upstream)
    results = (out, grad_in, grad_one, grad_two)
    out, grad_in, grad_one, grad_two = pl.pallas_call(
        placed,
        out_shape=tuple(jax.ShapeDtypeStruct(r.shape, r.dtype) for r in results),
        in_specs=[anywhere] * 4,
        out_specs=(anywhere,) * 4,
        scratch_shapes=[vmem(r.shape, r.dtype) for r in results] + [dma((10,)), dma((10,))],
    )(*results)
    return out.reshape(1, T, T, C), grad_in.reshape(1, T, T, C), by_input(grad_one), by_input(grad_two)


def solution(mesh):
    tile = P("dp", "ty", "tx", None)
    filters = P(None, None, None, "dp")
    plane = P("dp", "ty", "tx")
    sizes = (mesh.shape["dp"], mesh.shape["ty"], mesh.shape["tx"])
    return jax.shard_map(
        functools.partial(on_device, sizes),
        mesh=mesh,
        in_specs=(tile, filters, filters, plane, plane, P("dp", None), tile),
        out_specs=(tile, tile, filters, filters),
        check_vma=False,
    )
```

time: 64.2 us -> 54.5 us (0.85)
  local copies, waits for them, and re-layouts: 7.74 us -> 0 us
  Pallas kernels: 55.5 us -> 53.7 us
    unnamed x10 -> x0, local copies, waits for them, and re-layouts: 5.28 us -> none
    pallas_call x1, Pallas kernels: 55.5 us -> 51.2 us  [on_device(): pl.pallas_call(functools.partial(kernel, sizes, crop, scale), out_shape=(...]
    pallas_call x0 -> x1, Pallas kernels: none -> 2.52 us  [on_device(): pl.pallas_call(placed, out_shape=tuple((jax.ShapeDtypeStruct(r.shape, r.d...]
    slice x3 -> x0, local copies, waits for them, and re-layouts: 1.45 us -> none  [the longest x2 0.74 us: on_device(): grads[1]]
    reshape x1 -> x0, local copies, waits for them, and re-layouts: 1.01 us -> none  [on_device(): grads_t.reshape(2, C // n_dp, 9, C).transpose(0, 2, 3, 1)]
where the time goes in v1:
time: 54.5 us; the launch traced here: 54.3 us
  Pallas kernels  53.7 us (99%)
  between operations  0.64 us (1%)
    pallas_call x1, Pallas kernels, on_device(): pl.pallas_call(functools.partial(kernel, sizes, crop, scale), out_shape=(...  51.2 us
    pallas_call x1, Pallas kernels, on_device(): pl.pallas_call(placed, out_shape=tuple((jax.ShapeDtypeStruct(r.shape, r.d...  2.52 us

profile of v1, /device:TPU:1, one launch (start us, length us, event | category | flops | bytes accessed | tf_op | source)
XLA Modules:
  0.0 54.3 jit_solution(12337584791261301422)
XLA Ops:
  0.6 51.2 %shard_map.102 = (bf16[32,2,64,128]{3,2,1,0:T(8,128)(2,1)}, bf16[32,2,64,128]{3,2,1,0:T(8,128)(2,1)}, f32[9,32,128]{2,1,0:T(8,128)}, f32[9,32,128]{2,1,0:T(8,128)}) custom-call(bf16[1,64,64,128]{3,2,1,0:T(8,128)(2,1)} %features.1, bf16[9,32,128]{2,1,0:T(8,128)(2,1)} %bitcast.14, bf16[9,32,128]{2,1,0:T(8,128)(2,1)} %bitcast.15, f32[1,64,64]{2,1,0:T(8,128)} %speedup.1, ...), custom_call_target="tpu_custom_call" | custom-call | tf_op jit(solution)/shard_map/pallas_call | solution.py:553
  51.8 2.5 %shard_map.103 = (bf16[32,2,64,128]{3,2,1,0:T(8,128)(2,1)}, bf16[32,2,64,128]{3,2,1,0:T(8,128)(2,1)}, f32[9,32,128]{2,1,0:T(8,128)}, f32[9,32,128]{2,1,0:T(8,128)}) custom-call(bf16[32,2,64,128]{3,2,1,0:T(8,128)(2,1)} %get-tuple-element.12.refs_0_, bf16[32,2,64,128]{3,2,1,0:T(8,128)(2,1)} %get-tuple-element.13.refs_1_, ...), custom_call_target="tpu_custom_call" | custom-call | tf_op jit(solution)/shard_map/pallas_call | solution.py:569

commit v2 on v1

--- a/solution.py
+++ b/solution.py
@@ -32,8 +32,8 @@
     out, grad_in, grad_one, grad_two,
     raw, tails, colsend, colrecv, speed_v, mask_v, off_v, terrain, factor, wt, big,
     x_in, x_up, x_hid, x_gp, up_t, gp_t, pre, gh, rs, gf, gb, p1_recv, pieces_f, pieces_b, p2_recv,
-    z_slots, g_full, g_out, out_v,
-    local_sem, rows_s, rows_r, halo_s, halo_r, terr_s, terr_r, w_s, w_r, p1_s, p1_r, p2_s, p2_r, p4_s, p4_r, p5_s, p5_r, out_sem,
+    z_slots, g_full,
+    local_sem, rows_s, rows_r, halo_s, halo_r, terr_s, terr_r, w_s, w_r, share_s, share_r, p1_s, p1_r, p2_s, p2_r, p4_s, p4_r, p5_s, p5_r,
 ):
     n_dp, n_ty, n_tx = sizes
     n_x = 4
@@ -111,19 +111,41 @@
 
     pl.semaphore_wait(barrier, awaited)
 
+    half = rows // 2
+
     def w_copy(f, k):
-        return pltpu.make_async_remote_copy(
-            src_ref=filters[f], dst_ref=wt.at[f, :, own, :],
+        at = pl.ds(pl.multiple_of(core * half, half), half)
+        to = pl.ds(pl.multiple_of(dp * rows + core * half, half), half)
+        return pltpu.make_async_remote_copy(
+            src_ref=filters[f].at[:, at, :], dst_ref=wt.at[f, :, to, :],
             send_sem=w_s.at[f, k], recv_sem=w_r.at[f, k], device_id=dp_peers[k], device_id_type=MESH,
         )
 
+    def from_peer(k, which):
+        src = lax.rem(dp - (k + 1) + n_dp, n_dp)
+        return pl.ds(pl.multiple_of(src * rows + which * half, half), half)
+
     def w_arrival(f, k):
-        src = lax.rem(dp - (k + 1) + n_dp, n_dp)
-        theirs = pl.ds(pl.multiple_of(src * rows, rows), rows)
-        return pltpu.make_async_remote_copy(
-            src_ref=filters[f], dst_ref=wt.at[f, :, theirs, :],
+        return pltpu.make_async_remote_copy(
+            src_ref=filters[f].at[:, pl.ds(0, half), :], dst_ref=wt.at[f, :, from_peer(k, core), :],
             send_sem=w_s.at[f, k], recv_sem=w_r.at[f, k], device_id=dp_peers[k], device_id_type=MESH,
         )
+
+    def w_share(f, k, which):
+        at = wt.at[f, :, from_peer(k, which), :]
+        return pltpu.make_async_remote_copy(
+            src_ref=at, dst_ref=at,
+            send_sem=share_s.at[f, k], recv_sem=share_r.at[f, k], device_id=partner, device_id_type=MESH,
+        )
+
+    def share_filter(f):
+        for k in range(n_dp - 1):
+            w_arrival(f, k).wait_recv()
+            w_share(f, k, core).start()
+
+    def await_filter(f):
+        for k in range(n_dp - 1):
+            w_share(f, k, 1 - core).wait_recv()
 
     def rows_copy(i, n):
         dy = DIRS[i][0]
@@ -157,7 +179,15 @@
         )
 
     beside, above = (3, 4), (0, 1, 2, 5, 6, 7)
-    for i in (1, 6) + beside:
+    for k in range(n_dp - 1):
+        w_copy(0, k).start()
+    for i in beside:
+        @pl.when(inside(*DIRS[i]))
+        def _(i=i):
+            halo_copy(i).start()
+    for k in range(n_dp - 1):
+        w_copy(1, k).start()
+    for i in (1, 6):
         @pl.when(inside(*DIRS[i]))
         def _(i=i):
             for copy in rim_copies(i):
@@ -166,15 +196,11 @@
         @pl.when(inside(*d))
         def _(i=i):
             terr_copy(i).start()
-    for k in range(n_dp - 1):
-        w_copy(0, k).start()
     for i in (0, 2, 5, 7):
         @pl.when(inside(*DIRS[i]))
         def _(i=i):
             halo_copy(i).start()
 
-    for k in range(n_dp - 1):
-        w_copy(1, k).start()
 
     for dy, dx in DIRS:
         @pl.when(jnp.logical_not(inside(dy, dx)))
@@ -235,6 +261,8 @@
     await_rim(beside)
     fill_tails(2, T)
     lax.fori_loop(1, PAIRS, shifted, 0)
+    share_filter(0)
+
     for i, d in enumerate(DIRS):
         @pl.when(inside(-d[0], -d[1]))
         def _(i=i):
@@ -262,9 +290,9 @@
 
     loads[4].wait()
     loads[5].wait()
-    for k in range(n_dp - 1):
-        w_arrival(0, k).wait_recv()
+    await_filter(0)
     matrices(0, 0, False)
+    share_filter(1)
 
     def pair_conv(source, i, first, count, width):
         upper = source[pl.ds(first, count)].reshape(count * width, K)
@@ -289,8 +317,7 @@
             dest[q] = both[k * W:(k + 1) * W]
 
     main_conv(x_in, 0, pre)
-    for k in range(n_dp - 1):
-        w_arrival(1, k).wait_recv()
+    await_filter(1)
     matrices(1, 1, True)
     main_conv(x_up, 1, gh)
 
@@ -413,27 +440,23 @@
     matrices(2, 1, False)
     matrices(3, 0, True)
 
-    def rows_out(source, i, slot, first):
+    def rows_out(source, i, dest, first):
         def block(b, carry):
             y = pair_conv(source, i, 8 * b, 8, T).astype(BF16)
-            out_v[slot, pl.ds(8 * b, 8), 0] = y[:, 0:C].reshape(8, T, C)
-            out_v[slot, pl.ds(8 * b, 8), 1] = y[:, C:].reshape(8, T, C)
+            dest[pl.ds(8 * b, 8), 0] = y[:, 0:C].reshape(8, T, C)
+            dest[pl.ds(8 * b, 8), 1] = y[:, C:].reshape(8, T, C)
             return carry
 
         lax.fori_loop(first, first + 2, block, 0)
 
     on_core(0, p2_start)
     on_core(1, p4_start)
-    rows_out(x_hid, 2, 0, 0)
-    rows_out(x_hid, 2, 0, 2)
-    writes = [pltpu.make_async_copy(out_v.at[0], out, out_sem.at[0])]
-    writes[0].start()
+    rows_out(x_hid, 2, out, 0)
+    rows_out(x_hid, 2, out, 2)
     on_core(1, p5_start)
-    rows_out(x_gp, 3, 1, 0)
+    rows_out(x_gp, 3, grad_in, 0)
     on_core(0, p4_start)
-    rows_out(x_gp, 3, 1, 2)
-    writes.append(pltpu.make_async_copy(out_v.at[1], grad_in, out_sem.at[1]))
-    writes[1].start()
+    rows_out(x_gp, 3, grad_in, 2)
     on_core(0, p5_start)
 
     for k in range(len(mates)):
@@ -443,9 +466,7 @@
     for f, dest in enumerate((grad_one, grad_two)):
         for part in range(n_x):
             for k in range(9):
-                g_out[f, k, part * piece:(part + 1) * piece, :] = g_full[f, part, :, k * C:(k + 1) * C].astype(F32)
-        writes.append(pltpu.make_async_copy(g_out.at[f], dest, out_sem.at[2 + f]))
-        writes[-1].start()
+                dest[k, part * piece:(part + 1) * piece, :] = g_full[f, part, :, k * C:(k + 1) * C].astype(F32)
 
     for k in range(len(plane)):
         p2_copy(k).wait_send()
@@ -457,14 +478,13 @@
     for f in range(2):
         for k in range(n_dp - 1):
             w_copy(f, k).wait_send()
+            w_share(f, k, core).wait_send()
     for i, d in enumerate(DIRS):
         @pl.when(inside(*d))
         def _(i=i):
             terr_copy(i).wait_send()
             for copy in rim_copies(i):
                 copy.wait_send()
-    for copy in writes:
-        copy.wait()
 
 
 def by_output(filters):
@@ -476,24 +496,11 @@
 
 
 def placed(*refs):
-    sources, dests, held, (in_sem, out_sem) = refs[0:4], refs[4:8], refs[8:12], refs[12:14]
-    parts = []
-    for source, dest, mid in zip(sources, dests, held):
-        count = 4 if source.shape[0] % 4 == 0 else 1
-        step = source.shape[0] // count
-        parts += [(source, dest, mid, pl.ds(p * step, step)) for p in range(count)]
-    reads = [
-        pltpu.make_async_copy(source.at[at], mid.at[at], in_sem.at[i]) for i, (source, dest, mid, at) in enumerate(parts)
-    ]
-    writes = [
-        pltpu.make_async_copy(mid.at[at], dest.at[at], out_sem.at[i]) for i, (source, dest, mid, at) in enumerate(parts)
-    ]
-    for copy in reads:
+    sources, dests, sem = refs[0:4], refs[4:8], refs[8]
+    copies = [pltpu.make_async_copy(source, dest, sem.at[i]) for i, (source, dest) in enumerate(zip(sources, dests))]
+    for copy in copies:
         copy.start()
-    for read, write in zip(reads, writes):
-        read.wait()
-        write.start()
-    for copy in writes:
+    for copy in copies:
         copy.wait()
 
 
@@ -537,41 +544,39 @@
         vmem((n_plane, rows, TAPS), BF16),
         vmem((n_z, rows, TAPS), BF16),
         vmem((2, n_x, rows, TAPS), BF16),
-        vmem((2, 9, C // n_dp, C), F32),
-        vmem((2, T // 2, 2, T, C), BF16),
         dma((7,)),
         dma((2, 2)), dma((2, 2)),
         dma((8,)), dma((8,)),
         dma((8,)), dma((8,)),
         dma((2, n_dp - 1)), dma((2, n_dp - 1)),
+        dma((2, n_dp - 1)), dma((2, n_dp - 1)),
         dma, dma,
         dma((n_plane,)), dma((n_plane,)),
         dma((n_z - 1,)), dma((n_z - 1,)),
         dma((n_mates,)), dma((n_mates,)),
-        dma((4,)),
     ]
     out, grad_in, grad_one, grad_two = pl.pallas_call(
         functools.partial(kernel, sizes, crop, scale),
         out_shape=(
-            jax.ShapeDtypeStruct((T // 2, 2, T, C), BF16),
-            jax.ShapeDtypeStruct((T // 2, 2, T, C), BF16),
-            jax.ShapeDtypeStruct((9, C // n_dp, C), F32),
-            jax.ShapeDtypeStruct((9, C // n_dp, C), F32),
+            vmem((T // 2, 2, T, C), BF16),
+            vmem((T // 2, 2, T, C), BF16),
+            vmem((9, C // n_dp, C), F32),
+            vmem((9, C // n_dp, C), F32),
         ),
         in_specs=[anywhere] * 7,
-        out_specs=(anywhere,) * 4,
+        out_specs=(pl.BlockSpec(memory_space=vmem),) * 4,
         scratch_shapes=scratch,
         compiler_params=pltpu.CompilerParams(
-            collective_id=0, has_side_effects=True, vmem_limit_bytes=60 * 1024 * 1024
+            collective_id=0, has_side_effects=True, vmem_limit_bytes=52 * 1024 * 1024
         ),
     )(features, by_output(filter_one), by_output(filter_two), speedup, land_mask, offsets, upstream)
-    results = (out, grad_in, grad_one, grad_two)
+    results = [pltpu.with_memory_space_constraint(r, vmem) for r in (out, grad_in, grad_one, grad_two)]
     out, grad_in, grad_one, grad_two = pl.pallas_call(
         placed,
         out_shape=tuple(jax.ShapeDtypeStruct(r.shape, r.dtype) for r in results),
-        in_specs=[anywhere] * 4,
+        in_specs=[pl.BlockSpec(memory_space=vmem)] * 4,
         out_specs=(anywhere,) * 4,
-        scratch_shapes=[vmem(r.shape, r.dtype) for r in results] + [dma((10,)), dma((10,))],
+        scratch_shapes=[dma((4,))],
     )(*results)
     return out.reshape(1, T, T, C), grad_in.reshape(1, T, T, C), by_input(grad_one), by_input(grad_two)
 

time: 54.5 us -> 52.9 us (0.971)
  Pallas kernels: 53.7 us -> 52.2 us
    pallas_call x1, Pallas kernels: 2.52 us -> 1.44 us  [on_device(): pl.pallas_call(placed, out_shape=tuple((jax.ShapeDtypeStruct(r.shape, r.d...]
where the time goes in v2:
time: 52.9 us; the launch traced here: 52.8 us
  Pallas kernels  52.2 us (99%)
  between operations  0.64 us (1%)
    pallas_call x1, Pallas kernels, on_device(): pl.pallas_call(functools.partial(kernel, sizes, crop, scale), out_shape=(...  50.7 us
    pallas_call x1, Pallas kernels, on_device(): pl.pallas_call(placed, out_shape=tuple((jax.ShapeDtypeStruct(r.shape, r.d...  1.44 us

profile of v2, /device:TPU:1, one launch (start us, length us, event | category | flops | bytes accessed | tf_op | source)
XLA Modules:
  0.0 52.8 jit_solution(7671893227517740634)
XLA Ops:
  0.6 50.7 %shard_map.102 = (bf16[32,2,64,128]{3,2,1,0:T(8,128)(2,1)S(1)}, bf16[32,2,64,128]{3,2,1,0:T(8,128)(2,1)S(1)}, f32[9,32,128]{2,1,0:T(8,128)S(1)}, f32[9,32,128]{2,1,0:T(8,128)S(1)}) custom-call(bf16[1,64,64,128]{3,2,1,0:T(8,128)(2,1)} %features.1, bf16[9,32,128]{2,1,0:T(8,128)(2,1)} %bitcast.14, bf16[9,32,128]{2,1,0:T(8,128)(2,1)} %bitcast.15, ...), custom_call_target="tpu_custom_call" | custom-call | tf_op jit(solution)/shard_map/pallas_call | solution.py:558
  51.4 1.4 %shard_map.103 = (bf16[32,2,64,128]{3,2,1,0:T(8,128)(2,1)}, bf16[32,2,64,128]{3,2,1,0:T(8,128)(2,1)}, f32[9,32,128]{2,1,0:T(8,128)}, f32[9,32,128]{2,1,0:T(8,128)}) custom-call(bf16[32,2,64,128]{3,2,1,0:T(8,128)(2,1)S(1)} %get-tuple-element.12.refs_0_, bf16[32,2,64,128]{3,2,1,0:T(8,128)(2,1)S(1)} %get-tuple-element.13.refs_1_, ...), custom_call_target="tpu_custom_call" | custom-call | tf_op jit(solution)/shard_map/pallas_call | solution.py:574

commit v3 on v2

--- a/solution.py
+++ b/solution.py
@@ -53,21 +53,28 @@
             ok = okx if ok is None else jnp.logical_and(ok, okx)
         return ok
 
+    def away(k, n):
+        return min(k % n, n - k % n)
+
+    in_plane = sorted(range(1, n_dp * n_x), key=lambda k: -away(k // n_x, n_dp) - away(k, n_x))
+    along_z = sorted(range(1, n_z), key=lambda k: -away(k, n_z))
+    in_row = sorted(range(1, 2 * n_x), key=lambda k: -2 * away(k, n_x) - k // n_x)
+
     plane = [
         (lax.rem(dp + k // n_x, n_dp), ty, zl * n_x + lax.rem(x + k % n_x, n_x))
-        for k in range(1, n_dp * n_x)
+        for k in in_plane
     ]
 
     def z_peer(k):
         to = lax.rem(z + k, n_z)
         return (dp, (to // n_zl) * 2 + core, lax.rem(to, n_zl) * n_x + x)
 
-    z_peers = [z_peer(k) for k in range(1, n_z)]
+    z_peers = [z_peer(k) for k in along_z]
 
     def mate(k):
         return (dp, (ty // 2) * 2 + lax.rem(core + k // n_x, 2), zl * n_x + lax.rem(x + k % n_x, n_x))
 
-    mates = [mate(k) for k in range(1, 2 * n_x)]
+    mates = [mate(k) for k in in_row]
     partner = mate(n_x)
     dp_peers = [(lax.rem(dp + k, n_dp), ty, tx) for k in range(1, n_dp)]
 
@@ -402,7 +409,7 @@
 
     def p5_start():
         for k in range(len(z_peers)):
-            p4_copy(k, lax.rem(z - (k + 1) + n_z, n_z)).wait_recv()
+            p4_copy(k, lax.rem(z - along_z[k] + n_z, n_z)).wait_recv()
         total = z_slots[0].astype(F32)
         for k in range(1, n_z):
             total = total + z_slots[k].astype(F32)
@@ -460,7 +467,7 @@
     on_core(0, p5_start)
 
     for k in range(len(mates)):
-        dc, dx = (k + 1) // n_x, (k + 1) % n_x
+        dc, dx = in_row[k] // n_x, in_row[k] % n_x
         p5_copy(k, lax.rem(core + dc, 2), lax.rem(x - dx + n_x, n_x)).wait_recv()
     piece = C // (n_dp * n_x)
     for f, dest in enumerate((grad_one, grad_two)):

time: 52.9 us -> 51.8 us (0.979)
  Pallas kernels: 52.2 us -> 51.1 us
    pallas_call x1, Pallas kernels: 50.7 us -> 49.6 us  [on_device(): pl.pallas_call(functools.partial(kernel, sizes, crop, scale), out_shape=(...]
where the time goes in v3:
time: 51.8 us; the launch traced here: 51.7 us
  Pallas kernels  51.1 us (99%)
  between operations  0.64 us (1%)
    pallas_call x1, Pallas kernels, on_device(): pl.pallas_call(functools.partial(kernel, sizes, crop, scale), out_shape=(...  49.6 us
    pallas_call x1, Pallas kernels, on_device(): pl.pallas_call(placed, out_shape=tuple((jax.ShapeDtypeStruct(r.shape, r.d...  1.44 us

profile of v3, /device:TPU:1, one launch (start us, length us, event | category | flops | bytes accessed | tf_op | source)
XLA Modules:
  0.0 51.7 jit_solution(8867970450393537447)
XLA Ops:
  0.6 49.6 %shard_map.102 = (bf16[32,2,64,128]{3,2,1,0:T(8,128)(2,1)S(1)}, bf16[32,2,64,128]{3,2,1,0:T(8,128)(2,1)S(1)}, f32[9,32,128]{2,1,0:T(8,128)S(1)}, f32[9,32,128]{2,1,0:T(8,128)S(1)}) custom-call(bf16[1,64,64,128]{3,2,1,0:T(8,128)(2,1)} %features.1, bf16[9,32,128]{2,1,0:T(8,128)(2,1)} %bitcast.14, bf16[9,32,128]{2,1,0:T(8,128)(2,1)} %bitcast.15, ...), custom_call_target="tpu_custom_call" | custom-call | tf_op jit(solution)/shard_map/pallas_call | solution.py:565
  50.3 1.4 %shard_map.103 = (bf16[32,2,64,128]{3,2,1,0:T(8,128)(2,1)}, bf16[32,2,64,128]{3,2,1,0:T(8,128)(2,1)}, f32[9,32,128]{2,1,0:T(8,128)}, f32[9,32,128]{2,1,0:T(8,128)}) custom-call(bf16[32,2,64,128]{3,2,1,0:T(8,128)(2,1)S(1)} %get-tuple-element.12.refs_0_, bf16[32,2,64,128]{3,2,1,0:T(8,128)(2,1)S(1)} %get-tuple-element.13.refs_1_, ...), custom_call_target="tpu_custom_call" | custom-call | tf_op jit(solution)/shard_map/pallas_call | solution.py:581

commit v4 on v3

--- a/solution.py
+++ b/solution.py
@@ -192,6 +192,10 @@
         @pl.when(inside(*DIRS[i]))
         def _(i=i):
             halo_copy(i).start()
+    for i, d in enumerate(DIRS):
+        @pl.when(inside(*d))
+        def _(i=i):
+            terr_copy(i).start()
     for k in range(n_dp - 1):
         w_copy(1, k).start()
     for i in (1, 6):
@@ -199,10 +203,6 @@
         def _(i=i):
             for copy in rim_copies(i):
                 copy.start()
-    for i, d in enumerate(DIRS):
-        @pl.when(inside(*d))
-        def _(i=i):
-            terr_copy(i).start()
     for i in (0, 2, 5, 7):
         @pl.when(inside(*DIRS[i]))
         def _(i=i):

time: 51.8 us -> 50.8 us (0.981)
  Pallas kernels: 51.1 us -> 50.1 us
    pallas_call x1, Pallas kernels: 49.6 us -> 48.7 us  [on_device(): pl.pallas_call(functools.partial(kernel, sizes, crop, scale), out_shape=(...]
where the time goes in v4:
time: 50.8 us; the launch traced here: 50.7 us
  Pallas kernels  50.1 us (99%)
  between operations  0.64 us (1%)
    pallas_call x1, Pallas kernels, on_device(): pl.pallas_call(functools.partial(kernel, sizes, crop, scale), out_shape=(...  48.7 us
    pallas_call x1, Pallas kernels, on_device(): pl.pallas_call(placed, out_shape=tuple((jax.ShapeDtypeStruct(r.shape, r.d...  1.44 us

profile of v4, /device:TPU:1, one launch (start us, length us, event | category | flops | bytes accessed | tf_op | source)
XLA Modules:
  0.0 50.7 jit_solution(14224208157987292098)
XLA Ops:
  0.6 48.7 %shard_map.102 = (bf16[32,2,64,128]{3,2,1,0:T(8,128)(2,1)S(1)}, bf16[32,2,64,128]{3,2,1,0:T(8,128)(2,1)S(1)}, f32[9,32,128]{2,1,0:T(8,128)S(1)}, f32[9,32,128]{2,1,0:T(8,128)S(1)}) custom-call(bf16[1,64,64,128]{3,2,1,0:T(8,128)(2,1)} %features.1, bf16[9,32,128]{2,1,0:T(8,128)(2,1)} %bitcast.14, bf16[9,32,128]{2,1,0:T(8,128)(2,1)} %bitcast.15, ...), custom_call_target="tpu_custom_call" | custom-call | tf_op jit(solution)/shard_map/pallas_call | solution.py:565
  49.3 1.4 %shard_map.103 = (bf16[32,2,64,128]{3,2,1,0:T(8,128)(2,1)}, bf16[32,2,64,128]{3,2,1,0:T(8,128)(2,1)}, f32[9,32,128]{2,1,0:T(8,128)}, f32[9,32,128]{2,1,0:T(8,128)}) custom-call(bf16[32,2,64,128]{3,2,1,0:T(8,128)(2,1)S(1)} %get-tuple-element.12.refs_0_, bf16[32,2,64,128]{3,2,1,0:T(8,128)(2,1)S(1)} %get-tuple-element.13.refs_1_, ...), custom_call_target="tpu_custom_call" | custom-call | tf_op jit(solution)/shard_map/pallas_call | solution.py:581
